TPU v7x, 32 devices: a whole 2x2x4 slice. The times are simulated.
32 devices in a mesh: gz: 2 (over y), gy: 4 (over z), ta: 4 (over x, core).
Axes of the slice: x: 2, y: 2, z: 4, core: 2. Of those that a mesh axis runs over, the one named last changes fastest.
Arguments:
- movie: float32 [65536, 512], P(('gz', 'gy'), 'ta'), may hold values from 0 to 2
- traces: float32 [2048, 512], P(('gz', 'gy'), 'ta'), may hold values from 0.1 to 2
- entry_comp: int32 [512, 8], P(('gz', 'gy')), may hold values from 0 to 2048, as said below
- footprints: float32 [512, 8, 128], P(('gz', 'gy')), may hold values from 0.05 to 0.5
Outputs:
- traces_out: float32 [2048, 512], P(('gz', 'gy'), 'ta')
- footprints_out: float32 [512, 8, 128], P(('gz', 'gy'))
Inputs may be any that keep to these rules, and one draw needn't show every extreme that they name: `entry_comp`: the value 2048 marks an empty slot. In every tile the occupied slots come first; a tile holds up to 8 components, some tile holds 8 in every draw, and a component may appear in several tiles and blocks.
All inputs are finite; a program needn't handle non-finite values.
Results may differ from a plain program's by a relative error of at most 0.0001.
Values sent between devices are 32-bit elements; how exact they have to be, the bound alone decides.
A program may use at most 64 MiB of HBM per device.

v0:
```python
import functools

import jax
import jax.numpy as jnp
from jax import lax
from jax.experimental import pallas as pl
from jax.experimental.pallas import tpu as pltpu
from jax.sharding import PartitionSpec as P

ITERS = 2
RIDGE = 1.0
LANES = 128
MESH = pl.DeviceIdType.MESH
F32 = jnp.float32
BF16 = jnp.bfloat16
NT = (((1,), (1,)), ((), ()))
NN = (((1,), (0,)), ((), ()))


def split(x):
    hi = x.astype(BF16)
    return hi, (x - hi.astype(F32)).astype(BF16)


def dot(a, b, dims=NN):
    return lax.dot_general(a, b, dims, preferred_element_type=F32)


def exact(a, b, dims=NN):
    return lax.dot_general(a, b, dims, precision=lax.Precision.HIGHEST, preferred_element_type=F32)


def column(row):
    n = row.shape[1]
    r = lax.broadcasted_iota(jnp.int32, (n, n), 0)
    c = lax.broadcasted_iota(jnp.int32, (n, n), 1)
    return jnp.sum(jnp.where(r == c, jnp.broadcast_to(row, (n, n)), 0.0), axis=1, keepdims=True)


def kernel(
    G, Y, T, slots,
    movie_hbm, traces, comp, foot_in, tr_out, foot_out,
    mv, m2, mt, oh, oht, call, valid, foot, picked, own,
    half, curv, crow, proj, xs, nsend, nrecv, dsend, drecv, psend, precv,
    grad, dsp, grecv, dspr, gsum, dsps, grecv2, dspr2,
    load_sem, c_s, c_r, half_s, half_r, curv_s, curv_r, proj_s, proj_r,
    num_s, num_r, den_s, den_r, pick_s, pick_r, g1_s, g1_r, d1_s, d1_r, g2_s, g2_r, d2_s, d2_r, f_s, f_r,
):
    gz, gy, ta = lax.axis_index("gz"), lax.axis_index("gy"), lax.axis_index("ta")
    S, V = foot_in.shape
    R, F = traces.shape
    H = Y * R
    K = G * H
    NG = S // LANES
    TG = LANES // slots
    hb = S // 2
    hg = NG // 2
    pairs = T // 2
    core = lax.rem(ta, 2)
    pair = lax.div(ta, 2)
    mate = ta + 1 - 2 * core

    load = pltpu.make_async_copy(movie_hbm, mv, load_sem)
    load.start()

    def zpeer(d):
        return {"gz": lax.rem(gz + d, G)}

    def ypeer(d):
        return {"gy": lax.rem(gy + d, Y)}

    def tpeer(d):
        return {"ta": lax.rem(pair + d, pairs) * 2 + core}

    targets = [zpeer(d) for d in range(1, G)] + [ypeer(d) for d in range(1, Y)]
    targets += [tpeer(d) for d in range(1, pairs)] + [{"ta": mate}]
    barrier = pltpu.get_barrier_semaphore()
    for target in targets:
        pl.semaphore_signal(barrier, inc=1, device_id=target, device_id_type=MESH)
    pl.semaphore_wait(barrier, len(targets))

    sent = []

    def send(src, dst, ssem, rsem, target):
        copy = pltpu.make_async_remote_copy(
            src_ref=src, dst_ref=dst, send_sem=ssem, recv_sem=rsem, device_id=target, device_id_type=MESH
        )
        copy.start()
        sent.append(copy)
        return copy

    mine = pl.ds(pl.multiple_of(gy * R, R), R)

    def gather_half(step):
        return [
            send(own.at[step], half.at[step, mine], half_s.at[step, d], half_r.at[step, d], ypeer(d))
            for d in range(1, Y)
        ]

    own[0] = traces[...]
    waits_half = gather_half(0)
    call[0] = comp[...]
    waits_c = [send(call.at[0], call.at[d], c_s.at[d], c_r.at[d], zpeer(d)) for d in range(1, G)]

    for g in range(NG):
        rows = pl.ds(g * LANES, LANES)
        ok = (column(comp[g][0:1, :]) < float(K)).astype(F32)
        okb = jnp.broadcast_to(ok, (LANES, V))
        valid[rows, :] = okb
        foot[0, rows, :] = foot_in[rows, :] * okb

    load.wait()

    def split_tile(t, _):
        m = mv[pl.ds(pl.multiple_of(t * V, V), V), :]
        at = pl.ds(pl.multiple_of(t * V, V), V)
        hi, lo = split(m)
        m2[at, 0:F] = hi
        m2[at, F : 2 * F] = lo
        at = pl.ds(pl.multiple_of(t * F, F), F)
        hi, lo = split(m.T)
        mt[at, 0:V] = hi
        mt[at, V : 2 * V] = lo
        return _

    lax.fori_loop(0, NG * TG, split_tile, 0)

    blk_r = lax.broadcasted_iota(jnp.int32, (LANES, LANES), 0) // slots
    blk_c = lax.broadcasted_iota(jnp.int32, (LANES, LANES), 1) // slots
    same = blk_r == blk_c

    def tiles_dot(big, depth, g, rows):
        hi, lo = split(rows)
        w = jnp.concatenate(
            [jnp.concatenate([hi, hi], axis=1), jnp.concatenate([lo, lo], axis=1)], axis=0
        )
        at = pl.ds(pl.multiple_of(g * (TG * depth), TG * depth), TG * depth)
        res = dot(big[at, :], w, NT)
        res = res[:, 0:LANES] + res[:, LANES : 2 * LANES]
        acc = jnp.zeros((depth, LANES), F32)
        lane = lax.broadcasted_iota(jnp.int32, (depth, LANES), 1) // slots
        for t in range(TG):
            acc = jnp.where(lane == t, res[t * depth : (t + 1) * depth, :], acc)
        return acc.T

    def footgram(step, g):
        rows = pl.ds(pl.multiple_of(g * LANES, LANES), LANES)
        f = foot[step, rows, :]
        return jnp.where(same, exact(f, f, NT), 0.0)

    def curvature(step):
        def one(g, _):
            gram = footgram(step, g)
            curv[step, 0, g] = jnp.broadcast_to(jnp.sum(gram, axis=0, keepdims=True), (8, LANES))
            return _

        lax.fori_loop(0, NG, one, 0)
        return [
            send(curv.at[step, 0], curv.at[step, d], curv_s.at[step, d], curv_r.at[step, d], zpeer(d))
            for d in range(1, G)
        ]

    waits_curv = curvature(0)

    for w in waits_c:
        w.wait_recv()
    base = gz * H
    for d in range(G):
        for g in range(NG):
            row = call[d, g][0:1, :]
            cols = pl.ds((d * NG + g) * LANES, LANES)
            ids = (lax.broadcasted_iota(jnp.int32, (H, LANES), 0) + base).astype(F32)
            oht[:, cols] = jnp.where(ids == row, 1.0, 0.0).astype(BF16)
            ids = (lax.broadcasted_iota(jnp.int32, (LANES, H), 1) + base).astype(F32)
            oh[cols, :] = jnp.where(ids == column(row), 1.0, 0.0).astype(BF16)

    def pick(step, waits):
        half[step, mine, :] = own[step]
        for w in waits:
            w.wait_recv()
        hi, lo = split(half[step])
        both = jnp.concatenate([hi, lo], axis=1)
        out = []
        for d in list(range(1, G)) + [0]:
            res = dot(oh[pl.ds(d * S, S), :], both)
            res = res[:, 0:F] + res[:, F : 2 * F]
            if d:
                psend[step, d - 1] = res
                out.append(
                    send(
                        psend.at[step, d - 1], precv.at[step, d - 1],
                        pick_s.at[step, d], pick_r.at[step, d], zpeer(G - d),
                    )
                )
            else:
                total = res
        for d in range(1, G):
            out[d - 1].wait_recv()
            total = total + precv[step, d - 1]
        picked[...] = total

    pick(0, waits_half)

    for it in range(ITERS):
        def project(g, _, it=it):
            rows = pl.ds(pl.multiple_of(g * LANES, LANES), LANES)
            p = tiles_dot(mt, F, g, foot[it, rows, :])
            proj[it, 0, rows, :] = p - exact(footgram(it, g), picked[rows, :])
            return _

        lax.fori_loop(0, NG, project, 0)
        waits = [
            send(proj.at[it, 0], proj.at[it, d], proj_s.at[it, d], proj_r.at[it, d], zpeer(d))
            for d in range(1, G)
        ]
        for w in waits_curv:
            w.wait_recv()
        for d in range(G):
            for g in range(NG):
                hi, lo = split(curv[it, d, g])
                crow[:, (d * NG + g) * LANES : (d * NG + g + 1) * LANES] = jnp.concatenate([hi, lo], axis=0)
        for d in range(G):
            if d:
                waits[d - 1].wait_recv()
            hi, lo = split(proj[it, d])
            xs[pl.ds(d * S, S), 0:F] = hi
            xs[pl.ds(d * S, S), F : 2 * F] = lo
        waits = []
        for d in list(range(1, Y)) + [0]:
            to = lax.rem(gy + d, Y)
            block = oht[pl.ds(pl.multiple_of(to * R, R), R), :]
            num = dot(block, xs[...])
            num = num[:, 0:F] + num[:, F : 2 * F]
            den = dot(crow[...], block, NT)
            den = den[0:8] + den[8:16]
            if d:
                nsend[it, d - 1] = num
                dsend[it, d - 1] = den
                waits.append(
                    send(nsend.at[it, d - 1], nrecv.at[it, d - 1], num_s.at[it, d], num_r.at[it, d], ypeer(d))
                )
                waits.append(
                    send(dsend.at[it, d - 1], drecv.at[it, d - 1], den_s.at[it, d], den_r.at[it, d], ypeer(d))
                )
        for w in waits:
            w.wait_recv()
        for d in range(1, Y):
            num = num + nrecv[it, d - 1]
            den = den + drecv[it, d - 1]
        own[it + 1] = jnp.maximum(own[it] + num / (column(den[0:1, :]) + RIDGE), 0.0)
        pick(it + 1, gather_half(it + 1))

        def gradient(g, _, it=it):
            rows = pl.ds(pl.multiple_of(g * LANES, LANES), LANES)
            p = picked[rows, :]
            gram = jnp.where(same, exact(p, p, NT), 0.0)
            grad[it, rows, :] = tiles_dot(m2, V, g, p) - exact(gram, foot[it, rows, :])
            dsp[it, g] = jnp.broadcast_to(jnp.sum(gram, axis=0, keepdims=True), (8, LANES))
            return _

        lax.fori_loop(0, NG, gradient, 0)
        keep = pl.ds(pl.multiple_of(core * hb, hb), hb)
        give = pl.ds(pl.multiple_of((1 - core) * hb, hb), hb)
        a = send(grad.at[it, give], grecv.at[it], g1_s.at[it], g1_r.at[it], {"ta": mate})
        b = send(dsp.at[it, pl.ds((1 - core) * hg, hg)], dspr.at[it], d1_s.at[it], d1_r.at[it], {"ta": mate})
        a.wait_recv()
        b.wait_recv()
        gsum[it] = grad[it, keep, :] + grecv[it]
        dsps[it] = dsp[it, pl.ds(core * hg, hg)] + dspr[it]
        waits = []
        for d in range(1, pairs):
            waits.append(send(gsum.at[it], grecv2.at[it, d - 1], g2_s.at[it, d], g2_r.at[it, d], tpeer(d)))
            waits.append(send(dsps.at[it], dspr2.at[it, d - 1], d2_s.at[it, d], d2_r.at[it, d], tpeer(d)))
        for w in waits:
            w.wait_recv()
        gt, dt = gsum[it], dsps[it]
        for d in range(1, pairs):
            gt = gt + grecv2[it, d - 1]
            dt = dt + dspr2[it, d - 1]
        step = jnp.concatenate([column(dt[g][0:1, :]) for g in range(hg)], axis=0) + RIDGE
        foot[it + 1, keep, :] = jnp.maximum(foot[it, keep, :] + gt / step, 0.0) * valid[keep, :]
        a = send(foot.at[it + 1, keep], foot.at[it + 1, keep], f_s.at[it], f_r.at[it], {"ta": mate})
        if it == ITERS - 1:
            tr_out[...] = own[ITERS]
        a.wait_recv()
        if it < ITERS - 1:
            waits_curv = curvature(it + 1)
    foot_out[...] = foot[ITERS]
    for copy in sent:
        copy.wait_send()


def solution(mesh):
    G, Y, T = (mesh.shape[a] for a in ("gz", "gy", "ta"))

    def local(movie, traces, entry_comp, footprints):
        tiles, slots = entry_comp.shape
        V = footprints.shape[2]
        R, F = traces.shape
        S, H = tiles * slots, Y * R
        NG = S // LANES
        hb, hg, pairs = S // 2, NG // 2, T // 2
        comp = jnp.broadcast_to(entry_comp.astype(F32).reshape(NG, 1, LANES), (NG, 8, LANES))
        vm = pltpu.VMEM
        dma = pltpu.SemaphoreType.DMA
        I = ITERS
        np_ = max(pairs - 1, 1)
        scratch = [
            vm(movie.shape, F32), vm((tiles * V, 2 * F), BF16), vm((tiles * F, 2 * V), BF16),
            vm((G * S, H), BF16), vm((H, G * S), BF16), vm((G, NG, 8, LANES), F32),
            vm((S, V), F32), vm((I + 1, S, V), F32), vm((S, F), F32), vm((I + 1, R, F), F32),
            vm((I + 1, H, F), F32), vm((I, G, NG, 8, LANES), F32), vm((16, G * S), BF16),
            vm((I, G, S, F), F32), vm((G * S, 2 * F), BF16),
            vm((I, Y - 1, R, F), F32), vm((I, Y - 1, R, F), F32),
            vm((I, Y - 1, 8, R), F32), vm((I, Y - 1, 8, R), F32),
            vm((I + 1, G - 1, S, F), F32), vm((I + 1, G - 1, S, F), F32),
            vm((I, S, V), F32), vm((I, NG, 8, LANES), F32),
            vm((I, hb, V), F32), vm((I, hg, 8, LANES), F32), vm((I, hb, V), F32), vm((I, hg, 8, LANES), F32),
            vm((I, np_, hb, V), F32), vm((I, np_, hg, 8, LANES), F32),
            dma, dma((G,)), dma((G,)), dma((I + 1, Y)), dma((I + 1, Y)), dma((I, G)), dma((I, G)),
            dma((I, G)), dma((I, G)), dma((I, Y)), dma((I, Y)), dma((I, Y)), dma((I, Y)),
            dma((I + 1, G)), dma((I + 1, G)), dma((I,)), dma((I,)), dma((I,)), dma((I,)),
            dma((I, pairs)), dma((I, pairs)), dma((I, pairs)), dma((I, pairs)), dma((I,)), dma((I,)),
        ]
        vs = pl.BlockSpec(memory_space=pltpu.VMEM)
        tr, ft = pl.pallas_call(
            functools.partial(kernel, G, Y, T, slots),
            out_shape=(jax.ShapeDtypeStruct((R, F), F32), jax.ShapeDtypeStruct((S, V), F32)),
            in_specs=[pl.BlockSpec(memory_space=pl.ANY), vs, vs, vs],
            out_specs=(vs, vs),
            scratch_shapes=scratch,
            compiler_params=pltpu.CompilerParams(
                collective_id=0, has_side_effects=True, vmem_limit_bytes=56 * 1024 * 1024
            ),
        )(movie, traces, comp, footprints.reshape(S, V))
        return tr, ft.reshape(tiles, slots, V)

    placed = (
        P(("gz", "gy"), "ta"),
        P(("gz", "gy"), "ta"),
        P(("gz", "gy"), None),
        P(("gz", "gy"), None, None),
    )
    return jax.shard_map(
        local,
        mesh=mesh,
        in_specs=placed,
        out_specs=(P(("gz", "gy"), "ta"), P(("gz", "gy"), None, None)),
        check_vma=False,
    )
```

profile of v0, /device:TPU:27, one launch (start us, length us, event | category | flops | bytes accessed | tf_op | source)
XLA Modules:
  0.0 135.8 jit_solution(15286214341233243662)
XLA Ops:
  0.6 0.7 convert_element_type.3
  1.3 0.1 copy.6
  1.4 0.1 broadcast_in_dim.7
  1.5 0.6 broadcast_in_dim.8.comp
  2.1 130.4 %shard_map.59 = (f32[256,128]{1,0:T(8,128)}, f32[512,128]{1,0:T(8,128)}) custom-call(f32[8192,128]{1,0:T(8,128)} %movie_hbm.1, f32[256,128]{1,0:T(8,128)} %traces.1, f32[4,8,128]{2,1,0:T(8,128)} %broadcast_in_dim.8.comp, f32[512,128]{1,0:T(8,128)} %bitcast.2), custom_call_target="tpu_custom_call" | custom-call | tf_op jit(solution)/shard_map/pallas_call | solution.py:326
  132.5 1.6 %copy.9 = f32[256,128]{1,0:T(8,128)} copy(f32[256,128]{1,0:T(8,128)} %get-tuple-element.8) | data formatting | bytes 262144
  134.1 1.7 %copy.10 = f32[64,8,128]{2,1,0:T(8,128)} copy(f32[64,8,128]{2,1,0:T(8,128)} %bitcast.3) | data formatting | bytes 524288
where the time goes:
time: 136 us
  Pallas kernels  130 us (96%)
  local copies, waits for them, and re-layouts  4.03 us (3%)
    pallas_call x1, Pallas kernels, local(): pl.pallas_call(functools.partial(kernel, G, Y, T, slots), out_shape=(jax....  130 us
    unnamed x2, local copies, waits for them, and re-layouts  3.24 us

commit v1 on v0

v1 whole, which is shorter than its diff:
```python
import functools

import jax
import jax.numpy as jnp
from jax import lax
from jax.experimental import pallas as pl
from jax.experimental.pallas import tpu as pltpu
from jax.sharding import PartitionSpec as P

ITERS = 2
RIDGE = 1.0
LANES = 128
MESH = pl.DeviceIdType.MESH
F32 = jnp.float32
BF16 = jnp.bfloat16
NT = (((1,), (1,)), ((), ()))
NN = (((1,), (0,)), ((), ()))


def split(x):
    hi = x.astype(BF16)
    return hi, (x - hi.astype(F32)).astype(BF16)


def dot(a, b, dims=NN):
    return lax.dot_general(a, b, dims, preferred_element_type=F32)


def exact(a, b, dims=NN):
    return lax.dot_general(a, b, dims, precision=lax.Precision.HIGHEST, preferred_element_type=F32)


def column(row):
    n = row.shape[1]
    r = lax.broadcasted_iota(jnp.int32, (n, n), 0)
    c = lax.broadcasted_iota(jnp.int32, (n, n), 1)
    return jnp.sum(jnp.where(r == c, jnp.broadcast_to(row, (n, n)), 0.0), axis=1, keepdims=True)


def kernel(
    G, Y, T, slots,
    movie_hbm, traces, comp, foot_in, tr_out, foot_out,
    mv, m2, mt, oh, oht, oha, call, valid, foot, picked, own,
    full, curv, crow, xs, ysend, yrecv, acc, crecv,
    grad, dsp, grecv, dspr, gsum, dsps, grecv2, dspr2,
    load_sem, c_s, c_r, ch_s, ch_r, fy_s, fy_r, curv_s, curv_r,
    y_s, y_r, k_s, k_r, g1_s, g1_r, d1_s, d1_r, g2_s, g2_r, d2_s, d2_r, f_s, f_r,
):
    gz, gy, ta = lax.axis_index("gz"), lax.axis_index("gy"), lax.axis_index("ta")
    S, V = foot_in.shape
    R, F = traces.shape
    H = Y * R
    K = G * H
    NG = S // LANES
    TG = LANES // slots
    hb = S // 2
    hg = NG // 2
    pairs = T // 2
    core = lax.rem(ta, 2)
    pair = lax.div(ta, 2)
    mate = ta + 1 - 2 * core

    load = pltpu.make_async_copy(movie_hbm, mv, load_sem)
    load.start()

    def zpeer(d):
        return {"gz": lax.rem(gz + d, G)}

    def tpeer(d):
        return {"ta": lax.rem(pair + d, pairs) * 2 + core}

    others = [(d, e) for d in range(G) for e in range(Y) if d or e]

    def peer(d, e):
        return {"gz": lax.rem(gz + d, G), "gy": lax.rem(gy + e, Y)}

    targets = [peer(d, e) for d, e in others]
    targets += [tpeer(d) for d in range(1, pairs)] + [{"ta": mate}]
    barrier = pltpu.get_barrier_semaphore()
    for target in targets:
        pl.semaphore_signal(barrier, inc=1, device_id=target, device_id_type=MESH)
    pl.semaphore_wait(barrier, len(targets))

    ends = []

    def send(src, dst, ssem, rsem, target):
        copy = pltpu.make_async_remote_copy(
            src_ref=src, dst_ref=dst, send_sem=ssem, recv_sem=rsem, device_id=target, device_id_type=MESH
        )
        copy.start()
        ends.append(copy)
        return copy

    def landed(ref, sem):
        pltpu.make_async_remote_copy(
            src_ref=ref, dst_ref=ref, send_sem=sem, recv_sem=sem, device_id={"ta": mate}, device_id_type=MESH
        ).wait_recv()

    def descriptor(src, dst, ssem, rsem, target):
        return pltpu.make_async_remote_copy(
            src_ref=src, dst_ref=dst, send_sem=ssem, recv_sem=rsem, device_id=target, device_id_type=MESH
        )

    def along(step, way, b):
        ref = full.at[step, 0, b]
        return descriptor(ref, ref, ch_s.at[step, way, b], ch_r.at[step, way, b], {"gy": gy + 1 - 2 * way})

    def across(step, b):
        return [
            descriptor(full.at[step, 0, b], full.at[step, d, b], fy_s.at[step, d, b], fy_r.at[step, d, b], zpeer(d))
            for d in range(1, G)
        ]

    def more(way):
        return gy < Y - 1 if way == 0 else gy > 0

    def block_of(way, s):
        return gy - s if way == 0 else gy + s

    def inside(b):
        return jnp.logical_and(b >= 0, b < Y)

    def gather_start(step):
        full[step, 0, gy] = own[step]
        for way in (0, 1):
            pl.when(more(way))(lambda way=way: along(step, way, gy).start())
        for c in across(step, gy):
            c.start()

    def gather_stage(step, s):
        for way in (0, 1):
            b = block_of(way, s + 1)

            @pl.when(inside(b))
            def _(way=way, b=b):
                landed(full.at[step, 0, b], ch_r.at[step, way, b])
                pl.when(more(way))(lambda: along(step, way, b).start())
                for c in across(step, b):
                    c.start()

    def gather_end(step):
        for s in range(Y):
            for way in (0, 1):
                b = block_of(way, s)

                @pl.when(jnp.logical_and(inside(b), more(way)))
                def _(way=way, b=b):
                    along(step, way, b).wait_send()

        for b in range(Y):
            for c in across(step, b):
                c.wait_send()

    own[0] = traces[...]
    gather_start(0)
    call[0, 0] = comp[...]
    waits_c = [
        send(call.at[0, 0], call.at[d, e], c_s.at[d, e], c_r.at[d, e], peer(d, e)) for d, e in others
    ]

    for g in range(NG):
        rows = pl.ds(g * LANES, LANES)
        ok = (column(comp[g : g + 1, :]) < float(K)).astype(F32)
        okb = jnp.broadcast_to(ok, (LANES, V))
        valid[rows, :] = okb
        foot[0, rows, :] = foot_in[rows, :] * okb

    def split_tile(t, _):
        m = mv[pl.ds(pl.multiple_of(t * V, V), V), :]
        at = pl.ds(pl.multiple_of(t * V, V), V)
        hi, lo = split(m)
        m2[at, 0:F] = hi
        m2[at, F : 2 * F] = lo
        at = pl.ds(pl.multiple_of(t * F, F), F)
        hi, lo = split(m.T)
        mt[at, 0:V] = hi
        mt[at, V : 2 * V] = lo
        return _

    blk_r = lax.broadcasted_iota(jnp.int32, (LANES, LANES), 0) // slots
    blk_c = lax.broadcasted_iota(jnp.int32, (LANES, LANES), 1) // slots
    same = blk_r == blk_c

    def tiles_dot(big, depth, g, rows):
        hi, lo = split(rows)
        w = jnp.concatenate(
            [jnp.concatenate([hi, hi], axis=1), jnp.concatenate([lo, lo], axis=1)], axis=0
        )
        at = pl.ds(pl.multiple_of(g * (TG * depth), TG * depth), TG * depth)
        res = dot(big[at, :], w, NT)
        res = res[:, 0:LANES] + res[:, LANES : 2 * LANES]
        out = jnp.zeros((depth, LANES), F32)
        lane = lax.broadcasted_iota(jnp.int32, (depth, LANES), 1) // slots
        for t in range(TG):
            out = jnp.where(lane == t, res[t * depth : (t + 1) * depth, :], out)
        return out.T

    def footgram(step, g):
        rows = pl.ds(pl.multiple_of(g * LANES, LANES), LANES)
        f = foot[step, rows, :]
        return jnp.where(same, exact(f, f, NT), 0.0)

    def curvature(step):
        curv[step, 0, 0] = jnp.zeros_like(curv[step, 0, 0])
        for g in range(NG):
            curv[step, 0, 0, g : g + 1, :] = jnp.sum(footgram(step, g), axis=0, keepdims=True)
        return [
            send(curv.at[step, 0, 0], curv.at[step, d, e], curv_s.at[step, d, e], curv_r.at[step, d, e], peer(d, e))
            for d, e in others
        ]

    waits_curv = curvature(0)
    load.wait()
    tiles = NG * TG
    cuts = [tiles * i // Y for i in range(Y + 1)]
    for s in range(Y - 1):
        lax.fori_loop(cuts[s], cuts[s + 1], split_tile, 0)
        gather_stage(0, s)
    lax.fori_loop(cuts[Y - 1], cuts[Y], split_tile, 0)

    for g in range(NG):
        row = call[0, 0, g : g + 1, :]
        cols = pl.ds(g * LANES, LANES)
        ids = lax.broadcasted_iota(jnp.int32, (K, LANES), 0).astype(F32)
        oht[:, cols] = jnp.where(ids == row, 1.0, 0.0).astype(BF16)
        col = column(row)
        for d in range(G):
            ids = lax.broadcasted_iota(jnp.int32, (LANES, H), 1) + lax.rem(gz + G - d, G) * H
            oh[d, cols, :] = jnp.where(ids.astype(F32) == col, 1.0, 0.0).astype(BF16)

    def pick(step):
        total = jnp.zeros((S, F), F32)
        for d in range(G):
            if d:
                for b in range(Y):
                    landed(full.at[step, d, b], fy_r.at[step, d, b])
            hi, lo = split(full[step, d].reshape(H, F))
            res = dot(oh[d], jnp.concatenate([hi, lo], axis=1))
            total = total + res[:, 0:F] + res[:, F : 2 * F]
        picked[...] = total

    pick(0)
    for w in waits_c:
        w.wait_recv()
    first = (gz * Y + gy) * R
    every = [(0, 0)] + others
    for n, (d, e) in enumerate(every):
        for g in range(NG):
            ids = (lax.broadcasted_iota(jnp.int32, (R, LANES), 0) + first).astype(F32)
            hit = jnp.where(ids == call[d, e, g : g + 1, :], 1.0, 0.0)
            oha[:, pl.ds((n * NG + g) * LANES, LANES)] = hit.astype(BF16)

    upper = lax.div(2 * gy, Y)

    def order(i):
        down = Y - 1 - i - lax.div(gy + 1 + i, Y)
        up = i + lax.div(Y + i - gy, Y)
        return (1 - upper) * down + upper * up

    for it in range(ITERS):
        def project(g, _, it=it):
            rows = pl.ds(pl.multiple_of(g * LANES, LANES), LANES)
            p = tiles_dot(mt, F, g, foot[it, rows, :]) - exact(footgram(it, g), picked[rows, :])
            hi, lo = split(p)
            xs[rows, 0:F] = hi
            xs[rows, F : 2 * F] = lo
            return _

        lax.fori_loop(0, NG, project, 0)

        def partial(z, b):
            at = pl.ds(pl.multiple_of((z * Y + b) * R, R), R)
            num = dot(oht[at, :], xs[...])
            return num[:, 0:F] + num[:, F : 2 * F]

        blocks = [order(i) for i in range(Y - 1)] + [gy]
        for b in blocks:
            for d in range(1, G):
                ysend[it, d - 1, b] = partial(lax.rem(gz + d, G), b)
                send(ysend.at[it, d - 1, b], yrecv.at[it, d - 1, b], y_s.at[it, d, b], y_r.at[it, d, b], zpeer(d))
            acc[it, b] = partial(gz, b)

        def pass_on(b, it=it):
            up = lax.div(Y + b - gy - 1, Y)
            way = 1 - up
            came = gy + 1 - 2 * up
            total = acc[it, b]
            for d in range(1, G):
                landed(yrecv.at[it, d - 1, b], y_r.at[it, d, b])
                total = total + yrecv[it, d - 1, b]
            acc[it, b] = total

            @pl.when(inside(came))
            def _():
                landed(crecv.at[it, way, b], k_r.at[it, way, b])
                acc[it, b] = acc[it, b] + crecv[it, way, b]

            send(acc.at[it, b], crecv.at[it, way, b], k_s.at[it, b], k_r.at[it, way, b], {"gy": gy + 2 * up - 1})

        for b in blocks[: Y - 1]:
            pass_on(b)

        for w in waits_curv:
            w.wait_recv()
        for n, (d, e) in enumerate(every):
            for g in range(NG):
                hi, lo = split(jnp.broadcast_to(curv[it, d, e, g : g + 1, :], (8, LANES)))
                crow[:, (n * NG + g) * LANES : (n * NG + g + 1) * LANES] = jnp.concatenate([hi, lo], axis=0)
        den = dot(crow[...], oha[...], NT)
        den = column(den[0:1] + den[8:9]) + RIDGE

        for d in range(1, G):
            landed(yrecv.at[it, d - 1, gy], y_r.at[it, d, gy])
            acc[it, gy] = acc[it, gy] + yrecv[it, d - 1, gy]
        for way in (0, 1):

            @pl.when(more(1 - way))
            def _(way=way, it=it):
                landed(crecv.at[it, way, gy], k_r.at[it, way, gy])
                acc[it, gy] = acc[it, gy] + crecv[it, way, gy]

        own[it + 1] = jnp.maximum(own[it] + acc[it, gy] / den, 0.0)
        gather_start(it + 1)
        for s in range(Y - 1):
            gather_stage(it + 1, s)
        pick(it + 1)

        def gradient(g, _, it=it):
            rows = pl.ds(pl.multiple_of(g * LANES, LANES), LANES)
            p = picked[rows, :]
            gram = jnp.where(same, exact(p, p, NT), 0.0)
            grad[it, rows, :] = tiles_dot(m2, V, g, p) - exact(gram, foot[it, rows, :])
            dsp[it, g] = jnp.broadcast_to(jnp.sum(gram, axis=0, keepdims=True), (8, LANES))
            return _

        lax.fori_loop(0, NG, gradient, 0)
        keep = pl.ds(pl.multiple_of(core * hb, hb), hb)
        give = pl.ds(pl.multiple_of((1 - core) * hb, hb), hb)
        a = send(grad.at[it, give], grecv.at[it], g1_s.at[it], g1_r.at[it], {"ta": mate})
        b = send(dsp.at[it, pl.ds((1 - core) * hg, hg)], dspr.at[it], d1_s.at[it], d1_r.at[it], {"ta": mate})
        a.wait_recv()
        b.wait_recv()
        gsum[it] = grad[it, keep, :] + grecv[it]
        dsps[it] = dsp[it, pl.ds(core * hg, hg)] + dspr[it]
        waits = []
        for d in range(1, pairs):
            waits.append(send(gsum.at[it], grecv2.at[it, d - 1], g2_s.at[it, d], g2_r.at[it, d], tpeer(d)))
            waits.append(send(dsps.at[it], dspr2.at[it, d - 1], d2_s.at[it, d], d2_r.at[it, d], tpeer(d)))
        for w in waits:
            w.wait_recv()
        gt, dt = gsum[it], dsps[it]
        for d in range(1, pairs):
            gt = gt + grecv2[it, d - 1]
            dt = dt + dspr2[it, d - 1]
        step = jnp.concatenate([column(dt[g][0:1, :]) for g in range(hg)], axis=0) + RIDGE
        foot[it + 1, keep, :] = jnp.maximum(foot[it, keep, :] + gt / step, 0.0) * valid[keep, :]
        a = send(foot.at[it + 1, keep], foot.at[it + 1, keep], f_s.at[it], f_r.at[it], {"ta": mate})
        if it == ITERS - 1:
            tr_out[...] = own[ITERS]
        a.wait_recv()
        if it < ITERS - 1:
            waits_curv = curvature(it + 1)
    foot_out[...] = foot[ITERS]
    for step in range(ITERS + 1):
        gather_end(step)
    for copy in ends:
        copy.wait_send()


def solution(mesh):
    G, Y, T = (mesh.shape[a] for a in ("gz", "gy", "ta"))

    def local(movie, traces, entry_comp, footprints):
        tiles, slots = entry_comp.shape
        V = footprints.shape[2]
        R, F = traces.shape
        S, H = tiles * slots, Y * R
        NG = S // LANES
        hb, hg, pairs = S // 2, NG // 2, T // 2
        NP = -(-NG // 8) * 8
        comp = jnp.pad(entry_comp.astype(F32).reshape(NG, LANES), ((0, NP - NG), (0, 0)))
        vm = pltpu.VMEM
        dma = pltpu.SemaphoreType.DMA
        I = ITERS
        np_ = max(pairs - 1, 1)
        scratch = [
            vm(movie.shape, F32), vm((tiles * V, 2 * F), BF16), vm((tiles * F, 2 * V), BF16),
            vm((G, S, H), BF16), vm((G * H, S), BF16), vm((R, G * Y * S), BF16), vm((G, Y, NP, LANES), F32),
            vm((S, V), F32), vm((I + 1, S, V), F32), vm((S, F), F32), vm((I + 1, R, F), F32),
            vm((I + 1, G, Y, R, F), F32), vm((I, G, Y, NP, LANES), F32), vm((16, G * Y * S), BF16),
            vm((S, 2 * F), BF16), vm((I, G - 1, Y, R, F), F32), vm((I, G - 1, Y, R, F), F32),
            vm((I, Y, R, F), F32), vm((I, 2, Y, R, F), F32),
            vm((I, S, V), F32), vm((I, NG, 8, LANES), F32),
            vm((I, hb, V), F32), vm((I, hg, 8, LANES), F32), vm((I, hb, V), F32), vm((I, hg, 8, LANES), F32),
            vm((I, np_, hb, V), F32), vm((I, np_, hg, 8, LANES), F32),
            dma, dma((G, Y)), dma((G, Y)), dma((I + 1, 2, Y)), dma((I + 1, 2, Y)),
            dma((I + 1, G, Y)), dma((I + 1, G, Y)), dma((I, G, Y)), dma((I, G, Y)),
            dma((I, G, Y)), dma((I, G, Y)), dma((I, Y)), dma((I, 2, Y)),
            dma((I,)), dma((I,)), dma((I,)), dma((I,)),
            dma((I, pairs)), dma((I, pairs)), dma((I, pairs)), dma((I, pairs)), dma((I,)), dma((I,)),
        ]
        vs = pl.BlockSpec(memory_space=pltpu.VMEM)
        tr, ft = pl.pallas_call(
            functools.partial(kernel, G, Y, T, slots),
            out_shape=(jax.ShapeDtypeStruct((R, F), F32), jax.ShapeDtypeStruct((S, V), F32)),
            in_specs=[pl.BlockSpec(memory_space=pl.ANY), vs, vs, vs],
            out_specs=(vs, vs),
            scratch_shapes=scratch,
            compiler_params=pltpu.CompilerParams(
                collective_id=0, has_side_effects=True, vmem_limit_bytes=56 * 1024 * 1024
            ),
        )(movie, traces, comp, footprints.reshape(S, V))
        return tr, ft.reshape(tiles, slots, V)

    placed = (
        P(("gz", "gy"), "ta"),
        P(("gz", "gy"), "ta"),
        P(("gz", "gy"), None),
        P(("gz", "gy"), None, None),
    )
    return jax.shard_map(
        local,
        mesh=mesh,
        in_specs=placed,
        out_specs=(P(("gz", "gy"), "ta"), P(("gz", "gy"), None, None)),
        check_vma=False,
    )
```

time: 136 us -> 131 us (0.963)
  the two profiles are of different devices: /device:TPU:27 before, /device:TPU:0 now
where the time goes in v1:
time: 131 us
  Pallas kernels  125 us (95%)
  local copies, waits for them, and re-layouts  4.02 us (3%)
    pallas_call x1, Pallas kernels, local(): pl.pallas_call(functools.partial(kernel, G, Y, T, slots), out_shape=(jax....  125 us
    unnamed x2, local copies, waits for them, and re-layouts  3.24 us

profile of v1, /device:TPU:0, one launch (start us, length us, event | category | flops | bytes accessed | tf_op | source)
XLA Modules:
  0.0 130.7 jit_solution(13192358562566936729)
XLA Ops:
  0.6 0.7 convert_element_type.5
  1.3 0.1 copy.7
  1.4 0.1 reshape.13
  1.5 0.6 pad.4.comp
  2.1 125.4 %shard_map.59 = (f32[256,128]{1,0:T(8,128)}, f32[512,128]{1,0:T(8,128)}) custom-call(f32[8192,128]{1,0:T(8,128)} %movie_hbm.1, f32[256,128]{1,0:T(8,128)} %traces.1, f32[8,128]{1,0:T(8,128)} %pad.4.comp, f32[512,128]{1,0:T(8,128)} %bitcast.3), custom_call_target="tpu_custom_call" | custom-call | tf_op jit(solution)/shard_map/pallas_call | solution.py:403
  127.5 1.6 %copy.10 = f32[256,128]{1,0:T(8,128)} copy(f32[256,128]{1,0:T(8,128)} %get-tuple-element.8) | data formatting | bytes 262144
  129.1 1.7 %copy.11 = f32[64,8,128]{2,1,0:T(8,128)} copy(f32[64,8,128]{2,1,0:T(8,128)} %bitcast.2) | data formatting | bytes 524288
